TPU v7x, 256 devices: a whole 4x4x8 slice. The times are simulated.
256 devices in a mesh: frame: 32 (over z, y_hi, core), pix: 8 (over x, y_lo).
Axes of the slice: x: 4, y: 4 (y_hi: 2, y_lo: 2; y = y_hi * 2 + y_lo), z: 8, core: 2. Of those that a mesh axis runs over, the one named last changes fastest.
Arguments:
- library: float32 [12288, 3072], P('frame', 'pix'), may hold values from -5000 to 5000
- annulus: int32 [1536], P('pix'), may hold values from 0 to 383, as said below
Outputs:
- gram: float32 [12288, 12288], P('frame', 'pix')
Inputs may be any that keep to these rules, and one draw needn't show every extreme that they name: `annulus`: within each aligned block of 192 entries the values are distinct and rising, and each block holds both 0 and 383.
All inputs are finite; a program needn't handle non-finite values.
Results may differ from a plain program's by a relative error of at most 0.000065.
Values sent between devices are 32-bit elements; how exact they have to be, the bound alone decides.
A program may use at most 128 MiB of HBM per device.

v0:
```python
import jax
import jax.numpy as jnp
from jax import lax
from jax.sharding import PartitionSpec as P

PIX = 1536


def local(library, annulus):
    picked = jnp.take(library, annulus, axis=1)
    total = lax.psum(jnp.sum(picked, axis=1), "pix")
    frame_mean = total / PIX
    centered = picked - frame_mean[:, None]
    squares = lax.psum(jnp.sum(centered * centered, axis=1), "pix")
    unit = centered / jnp.sqrt(squares + 1e-06)[:, None]
    partial_gram = lax.dot_general(
        unit,
        lax.all_gather(unit, "frame", axis=0, tiled=True),
        (((1,), (1,)), ((), ())),
        precision=lax.Precision.HIGHEST,
        preferred_element_type=jnp.float32,
    )
    return lax.psum_scatter(partial_gram, "pix", scatter_dimension=1, tiled=True)


def solution(mesh):
    placed = (P("frame", "pix"), P("pix"))
    return jax.shard_map(
        local, mesh=mesh, in_specs=placed, out_specs=P("frame", "pix"), check_vma=False
    )
```

profile of v0, /device:TPU:1, one launch (start us, length us, event | category | flops | bytes accessed | tf_op | source)
XLA Modules:
  0.0 547.2 jit_solution(13108392722659654305)
XLA Ops:
  6.5 0.0 all-gather.2.cloned.1.call-start
  6.5 0.7 compare_and_fusion
  7.2 0.7 compare_select_fusion
  7.9 1.3 copy.3
  9.2 0.9 gather_fusion
  10.1 0.1 select_reduce_fusion
  10.2 16.8 %psum.14 = f32[384]{0:T(512)S(1)} all-reduce(f32[384]{0:T(512)S(1)} %select_reduce_fusion), channel_id=1, replica_groups=mesh['frame'=32,'pix'=8] {'pix'}, use_global_device_ids=true, to_apply=%region_1.2 | all-reduce | flops 384 | bytes 3072 | tf_op jit(solution)/shard_map/psum | solution.py:11
  27.0 0.1 multiply_reduce_fusion
  27.1 12.7 %psum.15 = f32[384]{0:T(512)S(1)} all-reduce(f32[384]{0:T(512)S(1)} %multiply_reduce_fusion), channel_id=1, replica_groups=mesh['frame'=32,'pix'=8] {'pix'}, use_global_device_ids=true, to_apply=%region_3.4 | all-reduce | flops 384 | bytes 3072 | tf_op jit(solution)/shard_map/psum | solution.py:14
  39.9 0.8 fusion.1
  40.7 0.0 all-gather.2.cloned.1.call-update
  40.7 0.0 reduce-scatter.2.cloned.1.call-start
  40.7 114.6 %all-gather.2.cloned.1.call-done = f32[12288,192]{0,1:T(8,128)} async-done(((f32[384,192]{0,1:T(8,128)}), f32[12288,192]{0,1:T(8,128)}) %all-gather.2.cloned.1.call-update) | async-done | bytes 9437200 | tf_op jit(solution)/shard_map/all_gather | solution.py:18
  155.4 20.4 %fusion = f32[384,12288]{1,0:T(8,128)} fusion(f32[12288,192]{0,1:T(8,128)} %all-gather.2.cloned.1.call-done, f32[192,384]{1,0:T(8,128)S(1)} %gather_fusion, f32[384]{0:T(512)S(1)} %add_sqrt_fusion, f32[384]{0:T(512)S(1)} %broadcast_multiply_fusion, pred[192]{0:T(512)(128)(4,1)S(1)} %compare_and_fusion), kind=kOutput, calls=%fused_computation.4 | convolution fusion | flops 10871857152 | bytes 28609728 | tf_op jit(solution)/shard_map/dot_general | solution.py:16
  175.8 0.0 reduce-scatter.2.cloned.1.call-update
  175.8 364.6 %reduce-scatter.2.cloned.1.call-done = f32[384,1536]{1,0:T(8,128)} async-done(((f32[384,12288]{1,0:T(8,128)}), f32[384,1536]{1,0:T(8,128)}) %reduce-scatter.2.cloned.1.call-update) | async-done | bytes 2359312 | tf_op jit(solution)/shard_map/reduce_scatter | solution.py:23
  (3 shorter events, 0.0 us)
Async XLA Ops:
  6.5 148.8 %all-gather.2.cloned.1.call-start = ((), (), s32[]{:S(2)}) async-start(), calls=%async_computation.1 | async-start | bytes 9732096 | tf_op jit(solution)/shard_map/all_gather | solution.py:18
  40.7 499.7 %reduce-scatter.2.cloned.1.call-start = ((), (), s32[]{:S(2)}) async-start(), calls=%async_computation.2 | async-start | bytes 21233664 | tf_op jit(solution)/shard_map/reduce_scatter | solution.py:23
Sparse Core Ops, SparseCore 0:
  40.8 114.5 all-gather.1
  175.9 364.4 reduce-scatter.1
where the time goes:
time: 547 us
  waiting for transfers between devices  479 us (88%)
  blocking collectives  29.5 us (5%)
  matrix products  20.4 us (4%)
  between operations  13.4 us (2%)
    reduce_scatter x1, waiting for transfers between devices, local(): lax.psum_scatter(partial_gram, 'pix', scatter_dimension=1, tiled=True)  365 us
    all_gather x1, waiting for transfers between devices, local(): lax.all_gather(unit, 'frame', axis=0, tiled=True)  115 us
    dot_general x1, matrix products, local(): lax.dot_general(unit, lax.all_gather(unit, 'frame', axis=0, tiled=True),...  20.4 us
    psum x1, blocking collectives, local(): total = lax.psum(jnp.sum(picked, axis=1), 'pix')  16.8 us
    psum x1, blocking collectives, local(): squares = lax.psum(jnp.sum(centered * centered, axis=1), 'pix')  12.7 us
  transfers between devices with their start and end apart: 2, of which 2 were waited for; matrix products, arithmetic and copies ran while one was open for 0% of the time, Pallas kernels for 0%

commit v1 on v0

v1 whole, which is shorter than its diff:
```python
import jax
import jax.numpy as jnp
from jax import lax
from jax.experimental import pallas as pl
from jax.experimental.pallas import tpu as pltpu
from jax.sharding import PartitionSpec as P

PIX = 1536
NZ = 8
NPIX = 8
SL = 24
ROWS = NZ * SL
FR = 384
NA = 4
EPS = 1e-06
MESH = pl.DeviceIdType.MESH
F32 = jnp.float32
BF16 = jnp.bfloat16


def device(x, y, z, c):
    return (z * 4 + (y // 2) * 2 + c, x * 2 + y % 2)


def split(v):
    hi = v.astype(BF16)
    return hi, (v - hi.astype(F32)).astype(BF16)


def dot(a, b):
    return lax.dot_general(a, b, (((1,), (0,)), ((), ())), preferred_element_type=F32)


def kernel(
    lib_ref, ann_ref, out_ref,
    piece, part, rows, cols, acc, mu, s1, s2, rmean, rscale,
    snd, scat, move, ag0, ag1, bex, rowsem, sibrow, outsem, outsnd,
):
    f = lax.axis_index("frame")
    p = lax.axis_index("pix")
    z, yh, c = f // 4, (f // 2) % 2, f % 2
    x, yl = p // 2, p % 2
    y = 2 * yh + yl

    def at(dx=0, dy=0, dz=0, dc=0):
        return device((x + dx) % 4, (y + dy) % 4, (z + dz) % NZ, (c + dc) % 2)

    sibling = at(dc=1)
    partner = at(dy=2)
    flip = device(x, 2 * yh + 1 - yl, z, c)
    pf = 2 * x + 1 - yl

    barrier = pltpu.get_barrier_semaphore()
    for d in range(1, NZ):
        pl.semaphore_signal(barrier, inc=1, device_id=at(dz=d), device_id_type=MESH)
    for dx in range(4):
        for dy in range(4):
            if dx or dy:
                pl.semaphore_signal(barrier, inc=1, device_id=at(dx, dy), device_id_type=MESH)
    pl.semaphore_signal(barrier, inc=1, device_id=sibling, device_id_type=MESH)

    band = lax.broadcasted_iota(jnp.int32, (FR, ROWS), 0)
    onehot = jnp.where(band == ann_ref[...], 1.0, 0.0).astype(F32).T.astype(BF16)
    lib = lib_ref[...]
    hi = lib.astype(BF16)
    rest = lib - hi.astype(F32)
    mid = rest.astype(BF16)
    low = (rest - mid.astype(F32)).astype(BF16)
    nt = (((1,), (1,)), ((), ()))
    picked = lax.dot_general(onehot, hi, nt, preferred_element_type=F32)
    picked += lax.dot_general(onehot, mid, nt, preferred_element_type=F32)
    picked += lax.dot_general(onehot, low, nt, preferred_element_type=F32)
    picked = picked.reshape(NZ, SL, FR)
    piece[...] = picked
    rows[c, :, p] = picked

    pl.semaphore_wait(barrier, 23)

    def send(src, dst, out, into, to):
        pltpu.make_async_remote_copy(
            src_ref=src, dst_ref=dst, send_sem=out, recv_sem=into, device_id=to, device_id_type=MESH
        ).start()

    def wait(like, sem):
        pltpu.make_async_copy(like, like, sem).wait()

    for d in (1, 7, 2, 6, 3, 5, 4):
        w = (z + d) % NZ
        send(piece.at[w], part.at[z], snd.at[0], scat.at[z], at(dz=d))

    send(piece, rows.at[c, :, p], snd.at[1], rowsem.at[p], flip)
    for d in (1, 3, 2):
        send(piece, rows.at[c, :, p], snd.at[1], rowsem.at[p], at(dx=d))
    send(piece, rows.at[c, :, p], snd.at[2], sibrow, sibling)

    def moves(d):
        w = (z + d) % NZ
        if d:
            wait(part.at[w], scat.at[w])
            src = part.at[w]
        else:
            src = piece.at[z]
        near = device(w // 2, w % 2 + 2 * yh, z, c)
        far = device(w // 2, w % 2 + 2 * (1 - yh), z, c)

        @pl.when(w == p)
        def _():
            pltpu.make_async_copy(src, cols.at[z, 0, p], move.at[0]).start()

        @pl.when(w != p)
        def _():
            send(src, cols.at[z, 0, p], snd.at[0], move.at[0], near)

        @pl.when(p < NA)
        def _():
            send(src, cols.at[z, 1, p], snd.at[3], move.at[1], far)

    for d in (0, 1, 7, 2, 6, 3, 5, 4):
        moves(d)

    wait(rows.at[c, :, pf], rowsem.at[pf])
    for d in (1, 3, 2):
        send(rows.at[c, :, pf], rows.at[c, :, pf], snd.at[1], rowsem.at[pf], at(dx=d))
    send(rows.at[c, :, pf], rows.at[c, :, pf], snd.at[2], sibrow, sibling)

    def forward0(j, d):
        send(cols.at[j, 0], cols.at[j, 0], snd.at[4], ag0.at[j], at(dz=d))

    def forward1(j, d):
        a = cols.at[j, 1, pl.ds(0, NA)]
        send(a, a, snd.at[5], ag1.at[j], at(dz=d))

    def cross(j):
        send(
            cols.at[j, 0, pl.ds(NA, NPIX - NA)], cols.at[j, 1, pl.ds(NA, NPIX - NA)],
            snd.at[6], bex.at[j], partner,
        )

    wait(cols.at[z, 0], move.at[0])
    forward0(z, 1)
    forward0(z, 7)
    cross(z)
    wait(cols.at[z, 1, pl.ds(0, NA)], move.at[1])
    forward1(z, 1)
    forward1(z, 7)

    def arrive(t):
        below, above = (z + NZ - t) % NZ, (z + t) % NZ
        if t == 4:
            wait(cols.at[above, 0], ag0.at[above])
            cross(above)
            wait(cols.at[above, 1, pl.ds(0, NA)], ag1.at[above])
            return
        for which, sem, fwd in ((0, ag0, forward0), (1, ag1, forward1)):
            for j, d, core in ((below, 1, 0), (above, 7, 1)):
                if which == 0:
                    wait(cols.at[j, 0], sem.at[j])
                else:
                    wait(cols.at[j, 1, pl.ds(0, NA)], sem.at[j])
                if t < 3:
                    fwd(j, d)
                else:
                    @pl.when(c == core)
                    def _():
                        fwd(j, d)
                if which == 0:
                    cross(j)

    def share(dx, q):
        k = 2 * ((x + dx) % 4) + q
        wait(rows.at[c, :, k], rowsem.at[k])
        send(rows.at[c, :, k], rows.at[c, :, k], snd.at[2], sibrow, sibling)

    arrive(1)
    for d in (1, 3, 2):
        share(d, yl)
    arrive(2)
    for d in (1, 3, 2):
        share(d, 1 - yl)
    arrive(3)
    wait(rows.at[0], sibrow)

    def block(ref, *idx):
        return ref[idx].reshape(ROWS, FR)

    for k in range(2):
        def add(j, tot):
            return tot + jnp.sum(block(rows, k, j), axis=0, keepdims=True)
        mean = lax.fori_loop(0, NZ, add, jnp.zeros((1, FR), F32)) / PIX
        def add2(j, tot):
            v = block(rows, k, j) - mean
            return tot + jnp.sum(v * v, axis=0, keepdims=True)
        sq = lax.fori_loop(0, NZ, add2, jnp.zeros((1, FR), F32))
        rmean[k] = mean
        rscale[k] = 1.0 / jnp.sqrt(sq + EPS)

    def product(j, first):
        if first is False:
            wait(cols.at[j, 1, pl.ds(NA, NPIX - NA)], bex.at[j])
        rhs = []
        for h in range(2):
            v = block(cols, j, h)
            if first:
                mu[h] = jnp.sum(v, axis=0, keepdims=True) / ROWS
            v = v - mu[h]
            one = jnp.sum(v, axis=0, keepdims=True)
            two = jnp.sum(v * v, axis=0, keepdims=True)
            if first:
                s1[h] = one
                s2[h] = two
            else:
                s1[h] += one
                s2[h] += two
            rhs.append(split(v))
        for k in range(2):
            u = (block(rows, k, j) - rmean[k]) * rscale[k]
            uhi, ulo = split(u)
            uhi, ulo = uhi.T, ulo.T
            for h in range(2):
                xhi, xlo = rhs[h]
                r = dot(uhi, xhi) + dot(uhi, xlo) + dot(ulo, xhi)
                if first:
                    acc[h, k] = r
                else:
                    acc[h, k] += r

    wait(cols.at[z, 1, pl.ds(NA, NPIX - NA)], bex.at[z])
    product(z, True)

    arrive(4)

    @pl.loop(1, NZ)
    def _(i):
        d = jnp.where(i % 2 == 1, (i + 1) // 2, NZ - i // 2)
        product((z + d) % NZ, False)

    copies = []
    for h in range(2):
        m = s1[h] / PIX
        sq = jnp.maximum(s2[h] - PIX * m * m, 0.0)
        r = 1.0 / jnp.sqrt(sq + EPS)
        col = pl.multiple_of((2 * (yh if h == 0 else 1 - yh) + c) * FR, 128)
        here = out_ref.at[:, pl.ds(col, FR)]
        acc[h, 1 - c] = acc[h, 1 - c] * r
        theirs = pltpu.make_async_remote_copy(
            src_ref=acc.at[h, 1 - c], dst_ref=here, send_sem=outsnd.at[h], recv_sem=outsem.at[h],
            device_id=sibling, device_id_type=MESH,
        )
        theirs.start()
        acc[h, c] = acc[h, c] * r
        mine = pltpu.make_async_copy(acc.at[h, c], here, outsnd.at[2 + h])
        mine.start()
        copies.append((theirs, mine))
    for theirs, mine in copies:
        theirs.wait()
        mine.wait()

    wait(cols.at[pl.ds(0, 7), 0, pl.ds(0, 2)], snd.at[0])
    wait(cols.at[pl.ds(0, 7), 0], snd.at[1])
    wait(cols.at[:, 0], snd.at[2])

    @pl.when(p < NA)
    def _():
        wait(cols.at[0, 0], snd.at[3])

    wait(cols.at[pl.ds(0, 7), 0], snd.at[4])
    wait(cols.at[pl.ds(0, 7), 0, pl.ds(0, NA)], snd.at[5])
    wait(cols.at[:, 0, pl.ds(0, NPIX - NA)], snd.at[6])


def local(library, annulus):
    dma = pltpu.SemaphoreType.DMA
    return pl.pallas_call(
        kernel,
        out_shape=jax.ShapeDtypeStruct((FR, 4 * FR), F32),
        in_specs=[pl.BlockSpec(memory_space=pltpu.VMEM)] * 2,
        out_specs=pl.BlockSpec(memory_space=pl.ANY),
        scratch_shapes=[
            pltpu.VMEM((NZ, SL, FR), F32),
            pltpu.VMEM((NZ, SL, FR), F32),
            pltpu.VMEM((2, NZ, NPIX, SL, FR), F32),
            pltpu.VMEM((NZ, 2, NPIX, SL, FR), F32),
            pltpu.VMEM((2, 2, FR, FR), F32),
            pltpu.VMEM((2, 1, FR), F32),
            pltpu.VMEM((2, 1, FR), F32),
            pltpu.VMEM((2, 1, FR), F32),
            pltpu.VMEM((2, 1, FR), F32),
            pltpu.VMEM((2, 1, FR), F32),
            dma((7,)),
            dma((NZ,)),
            dma((2,)),
            dma((NZ,)),
            dma((NZ,)),
            dma((NZ,)),
            dma((NPIX,)),
            dma,
            dma((2,)),
            dma((4,)),
        ],
        compiler_params=pltpu.CompilerParams(
            collective_id=0, has_side_effects=True, vmem_limit_bytes=48 * 2**20
        ),
    )(library, annulus.reshape(1, ROWS))


def solution(mesh):
    placed = (P("frame", "pix"), P("pix"))
    return jax.shard_map(
        local, mesh=mesh, in_specs=placed, out_specs=P("frame", "pix"), check_vma=False
    )
```

time: 547 us -> 81.9 us (0.15)
  waiting for transfers between devices: 479 us -> 0 us
  Pallas kernels: 0 us -> 78.1 us
  blocking collectives: 29.5 us -> 0 us
  matrix products: 20.4 us -> 0 us
  between operations: 13.4 us -> 0.01 us
    reduce_scatter x1 -> x0, waiting for transfers between devices: 365 us -> none  [local(): lax.psum_scatter(partial_gram, 'pix', scatter_dimension=1, tiled=True)]
    all_gather x1 -> x0, waiting for transfers between devices: 115 us -> none  [local(): lax.all_gather(unit, 'frame', axis=0, tiled=True)]
    pallas_call x0 -> x1, Pallas kernels: none -> 78.1 us  [local(): pl.pallas_call(kernel, out_shape=jax.ShapeDtypeStruct((FR, 4 * FR), F32),...]
    psum x2 -> x0, blocking collectives: 29.5 us -> none  [the longest x1 16.8 us: local(): total = lax.psum(jnp.sum(picked, axis=1), 'pix')]
    dot_general x1 -> x0, matrix products: 20.4 us -> none  [local(): lax.dot_general(unit, lax.all_gather(unit, 'frame', axis=0, tiled=True),...]
  transfers between devices with their start and end apart: 2 -> 0, of which waited for: 2 -> 0; matrix products, arithmetic and copies ran while one was open for 0% -> 0% of each run, Pallas kernels for 0% -> 0%
where the time goes in v1:
time: 81.9 us; the launch traced here: 81.2 us
  Pallas kernels  78.1 us (95%)
  local copies, waits for them, and re-layouts  3.15 us (4%)
    pallas_call x1, Pallas kernels, local(): pl.pallas_call(kernel, out_shape=jax.ShapeDtypeStruct((FR, 4 * FR), F32),...  78.1 us
    unnamed x5, local copies, waits for them, and re-layouts  3.15 us

profile of v1, /device:TPU:1, one launch (start us, length us, event | category | flops | bytes accessed | tf_op | source)
XLA Modules:
  0.0 81.2 jit_solution(8465993279207075767)
XLA Ops:
  0.0 0.0 copy-start
  0.0 1.1 %copy-done = f32[384,384]{1,0:T(8,128)S(1)} copy-done((f32[384,384]{1,0:T(8,128)S(1)}, f32[384,384]{1,0:T(8,128)}, u32[]{:S(2)}) %copy-start) | copy-done | bytes 589848
  1.1 0.0 copy-start.1
  1.1 0.7 copy-done.1
  1.7 78.1 %shard_map.28 = f32[384,1536]{1,0:T(8,128)S(1)} custom-call(f32[384,384]{1,0:T(8,128)S(1)} %copy-done, s32[1,192]{1,0:T(1,128)S(1)} %bitcast.1), custom_call_target="tpu_custom_call" | custom-call | tf_op jit(solution)/shard_map/pallas_call | solution.py:273
  79.8 1.4 %copy.4 = f32[384,1536]{1,0:T(8,128)} copy(f32[384,1536]{1,0:T(8,128)S(1)} %shard_map.28) | data formatting | bytes 4718592
Async XLA Ops:
  0.0 1.1 %copy-start = (f32[384,384]{1,0:T(8,128)S(1)}, f32[384,384]{1,0:T(8,128)}, u32[]{:S(2)}) copy-start(f32[384,384]{1,0:T(8,128)} %lib_ref.1) | copy-start | bytes 1769476
  1.1 0.7 copy-start.1

commit v2 on v1

v2 whole, which is shorter than its diff:
```python
import jax
import jax.numpy as jnp
from jax import lax
from jax.experimental import pallas as pl
from jax.experimental.pallas import tpu as pltpu
from jax.sharding import PartitionSpec as P

PIX = 1536
NZ = 8
NPIX = 8
SL = 24
ROWS = NZ * SL
FR = 384
NA = 4
EPS = 1e-06
MESH = pl.DeviceIdType.MESH
F32 = jnp.float32
BF16 = jnp.bfloat16


def device(x, y, z, c):
    return (z * 4 + (y // 2) * 2 + c, x * 2 + y % 2)


def split(v):
    hi = v.astype(BF16)
    return hi, (v - hi.astype(F32)).astype(BF16)


def dot(a, b):
    return lax.dot_general(a, b, (((1,), (0,)), ((), ())), preferred_element_type=F32)


def kernel(
    lib_ref, ann_ref, out_ref,
    piece, rows, cols, acc, mu, s1, s2, rmean, rscale,
    snd, move, ag0, ag1, bex, rowsem, rowlow, sibrow, outsem, outsnd,
):
    f = lax.axis_index("frame")
    p = lax.axis_index("pix")
    z, yh, c = f // 4, (f // 2) % 2, f % 2
    x, yl = p // 2, p % 2
    y = 2 * yh + yl

    def at(dx=0, dy=0, dz=0, dc=0):
        return device((x + dx) % 4, (y + dy) % 4, (z + dz) % NZ, (c + dc) % 2)

    sibling = at(dc=1)
    partner = at(dy=2)
    flip = device(x, 2 * yh + 1 - yl, z, c)
    pf = 2 * x + 1 - yl

    barrier = pltpu.get_barrier_semaphore()
    def greet(to):
        pl.semaphore_signal(barrier, inc=1, device_id=to, device_id_type=MESH)

    def target(w):
        return device(z // 2, z % 2 + 2 * yh, w, c)

    for to in (at(dz=1), at(dz=7), at(dx=1), at(dx=3), flip, partner, sibling):
        greet(to)
    for w in range(NZ):
        @pl.when((w != z) | (z != p))
        def _():
            greet(target(w))
    for k in range(NPIX):
        @pl.when((k != p) | (z != p))
        def _():
            greet(device(k // 2, 2 * yh + k % 2, p, c))

    band = lax.broadcasted_iota(jnp.int32, (FR, ROWS), 0)
    onehot = jnp.where(band == ann_ref[...], 1.0, 0.0).astype(F32).T.astype(BF16)
    lib = lib_ref[...]
    hi = lib.astype(BF16)
    rest = lib - hi.astype(F32)
    mid = rest.astype(BF16)
    low = (rest - mid.astype(F32)).astype(BF16)
    nt = (((1,), (1,)), ((), ()))
    picked = lax.dot_general(onehot, hi, nt, preferred_element_type=F32)
    picked += lax.dot_general(onehot, mid, nt, preferred_element_type=F32)
    picked += lax.dot_general(onehot, low, nt, preferred_element_type=F32)
    picked = picked.reshape(NZ, SL, FR)
    piece[...] = picked
    rows[c, :, p] = picked

    pl.semaphore_wait(barrier, 7 + 2 * NZ - jnp.where(z == p, 2, 0))

    def send(src, dst, out, into, to):
        pltpu.make_async_remote_copy(
            src_ref=src, dst_ref=dst, send_sem=out, recv_sem=into, device_id=to, device_id_type=MESH
        ).start()

    def wait(like, sem):
        pltpu.make_async_copy(like, like, sem).wait()

    def scatter():
        for d in (4, 3, 5, 2, 6, 1, 7):
            w = (z + d) % NZ
            send(piece.at[w], cols.at[w, 0, p], snd.at[0], move, target(w))

        @pl.when(z != p)
        def _():
            send(piece.at[z], cols.at[z, 0, p], snd.at[0], move, target(z))

        @pl.when(z == p)
        def _():
            pltpu.make_async_copy(piece.at[z], cols.at[z, 0, p], move).start()

    def own(j):
        return cols.at[j, 0]

    def also(j):
        return cols.at[j, 1, pl.ds(0, NA)]

    def forward0(j, d):
        send(own(j), own(j), snd.at[4], ag0.at[j], at(dz=d))

    def forward1(j, d):
        send(also(j), also(j), snd.at[5], ag1.at[j], at(dz=d))

    def cross(j):
        rest = pl.ds(NA, NPIX - NA)
        send(cols.at[j, 0, rest], cols.at[j, 1, rest], snd.at[6], bex.at[j], partner)

    def begin():
        wait(own(z), move)
        forward0(z, 1)
        forward0(z, 7)
        send(cols.at[z, 0, pl.ds(0, NA)], also(z), snd.at[3], ag1.at[z], partner)
        cross(z)
        wait(also(z), ag1.at[z])
        forward1(z, 1)
        forward1(z, 7)

    def arrive(t):
        below, above = (z + NZ - t) % NZ, (z + t) % NZ
        for view, sem, fwd in ((own, ag0, forward0), (also, ag1, forward1)):
            for j, d, core in ((below, 1, 0), (above, 7, 1)):
                wait(view(j), sem.at[j])
                if t < 3:
                    fwd(j, d)
                else:
                    @pl.when(c == core)
                    def _():
                        fwd(j, d)
                if view is own:
                    cross(j)

    def row(k):
        return rows.at[c, :, k]

    def share(k):
        send(row(k), row(k), snd.at[2], sibrow, sibling)

    def both(src, k):
        for d in (1, 3):
            send(src, row(k), snd.at[1], rowsem.at[k], at(dx=d))

    def pass_on(q):
        left, right = 2 * ((x + 3) % 4) + q, 2 * ((x + 1) % 4) + q
        wait(row(left), rowsem.at[left])
        top = rows.at[c, pl.ds(0, 4), left]
        send(top, top, snd.at[1], rowsem.at[left], at(dx=1))
        share(left)
        wait(row(right), rowsem.at[right])
        low = rows.at[c, pl.ds(4, 4), right]
        send(low, low, snd.at[1], rowlow.at[right], at(dx=3))
        share(right)

    def last(q):
        k = 2 * ((x + 2) % 4) + q
        wait(rows.at[c, pl.ds(0, 4), k], rowsem.at[k])
        wait(rows.at[c, pl.ds(4, 4), k], rowlow.at[k])
        share(k)

    scatter()
    send(piece, row(p), snd.at[1], rowsem.at[p], flip)
    both(piece, p)
    send(piece, row(p), snd.at[2], sibrow, sibling)
    begin()
    wait(row(pf), rowsem.at[pf])
    both(row(pf), pf)
    share(pf)
    pass_on(yl)
    arrive(1)
    pass_on(1 - yl)
    last(yl)
    arrive(2)
    last(1 - yl)
    wait(rows.at[0], sibrow)

    def block(ref, *idx):
        return ref[idx].reshape(ROWS, FR)

    for k in range(2):
        def add(j, tot):
            return tot + jnp.sum(block(rows, k, j), axis=0, keepdims=True)
        mean = lax.fori_loop(0, NZ, add, jnp.zeros((1, FR), F32)) / PIX
        def add2(j, tot):
            v = block(rows, k, j) - mean
            return tot + jnp.sum(v * v, axis=0, keepdims=True)
        sq = lax.fori_loop(0, NZ, add2, jnp.zeros((1, FR), F32))
        rmean[k] = mean
        rscale[k] = 1.0 / jnp.sqrt(sq + EPS)

    def shifted(j, h, first):
        v = block(cols, j, h)
        if first:
            mu[h] = jnp.sum(v, axis=0, keepdims=True) / ROWS
        v = v - mu[h]
        one = jnp.sum(v, axis=0, keepdims=True)
        two = jnp.sum(v * v, axis=0, keepdims=True)
        s1[h] = one if first else s1[h] + one
        s2[h] = two if first else s2[h] + two
        return split(v)

    def product(j, hs, first=False):
        if 1 in hs:
            wait(cols.at[j, 1, pl.ds(NA, NPIX - NA)], bex.at[j])
        pairs = [shifted(j, h, first) for h in hs]
        xhi, xlo = (jnp.concatenate(v, axis=1) for v in zip(*pairs))
        for k in range(2):
            u = (block(rows, k, j) - rmean[k]) * rscale[k]
            uhi, ulo = split(u)
            uhi, ulo = uhi.T, ulo.T
            r = dot(uhi, xhi) + dot(uhi, xlo) + dot(ulo, xhi)
            for i, h in enumerate(hs):
                r_h = r[:, i * FR : (i + 1) * FR]
                acc[h, k] = r_h if first else acc[h, k] + r_h

    def pair(t):
        @pl.loop(0, 2)
        def _(i):
            product((z + jnp.where(i == 0, t, NZ - t)) % NZ, (0, 1))

    copies = []

    def output(h):
        m = s1[h] / PIX
        sq = jnp.maximum(s2[h] - PIX * m * m, 0.0)
        r = 1.0 / jnp.sqrt(sq + EPS)
        col = pl.multiple_of((2 * (yh if h == 0 else 1 - yh) + c) * FR, 128)
        here = out_ref.at[:, pl.ds(col, FR)]
        acc[h, 1 - c] = acc[h, 1 - c] * r
        theirs = pltpu.make_async_remote_copy(
            src_ref=acc.at[h, 1 - c], dst_ref=here, send_sem=outsnd.at[h], recv_sem=outsem.at[h],
            device_id=sibling, device_id_type=MESH,
        )
        theirs.start()
        acc[h, c] = acc[h, c] * r
        mine = pltpu.make_async_copy(acc.at[h, c], here, outsnd.at[2 + h])
        mine.start()
        copies.append((theirs, mine))

    far = (z + 4) % NZ
    product(z, (0, 1), True)
    pair(1)
    arrive(3)
    pair(2)
    wait(own(far), ag0.at[far])
    cross(far)
    pair(3)
    product(far, (0,))
    output(0)
    wait(also(far), ag1.at[far])
    product(far, (1,))
    output(1)
    for theirs, mine in copies:
        theirs.wait()
        mine.wait()

    wait(cols.at[0, 0, pl.ds(0, 7)], snd.at[0])

    @pl.when(z != p)
    def _():
        wait(piece.at[0], snd.at[0])

    wait(cols.at[pl.ds(0, 7), 0], snd.at[1])
    wait(cols.at[:, 0], snd.at[2])

    wait(also(0), snd.at[3])
    wait(cols.at[pl.ds(0, 7), 0], snd.at[4])
    wait(cols.at[pl.ds(0, 7), 0, pl.ds(0, NA)], snd.at[5])
    wait(cols.at[:, 0, pl.ds(0, NPIX - NA)], snd.at[6])


def local(library, annulus):
    dma = pltpu.SemaphoreType.DMA
    return pl.pallas_call(
        kernel,
        out_shape=jax.ShapeDtypeStruct((FR, 4 * FR), F32),
        in_specs=[pl.BlockSpec(memory_space=pltpu.VMEM)] * 2,
        out_specs=pl.BlockSpec(memory_space=pl.ANY),
        scratch_shapes=[
            pltpu.VMEM((NZ, SL, FR), F32),
            pltpu.VMEM((2, NZ, NPIX, SL, FR), F32),
            pltpu.VMEM((NZ, 2, NPIX, SL, FR), F32),
            pltpu.VMEM((2, 2, FR, FR), F32),
            pltpu.VMEM((2, 1, FR), F32),
            pltpu.VMEM((2, 1, FR), F32),
            pltpu.VMEM((2, 1, FR), F32),
            pltpu.VMEM((2, 1, FR), F32),
            pltpu.VMEM((2, 1, FR), F32),
            dma((7,)),
            dma,
            dma((NZ,)),
            dma((NZ,)),
            dma((NZ,)),
            dma((NPIX,)),
            dma((NPIX,)),
            dma,
            dma((2,)),
            dma((4,)),
        ],
        compiler_params=pltpu.CompilerParams(
            collective_id=0, has_side_effects=True, vmem_limit_bytes=48 * 2**20
        ),
    )(library, annulus.reshape(1, ROWS))


def solution(mesh):
    placed = (P("frame", "pix"), P("pix"))
    return jax.shard_map(
        local, mesh=mesh, in_specs=placed, out_specs=P("frame", "pix"), check_vma=False
    )
```

time: 81.9 us -> 70.3 us (0.86)
  Pallas kernels: 78.1 us -> 67 us
    pallas_call x1, Pallas kernels: 78.1 us -> 67 us  [local(): pl.pallas_call(kernel, out_shape=jax.ShapeDtypeStruct((FR, 4 * FR), F32),...]
where the time goes in v2:
time: 70.3 us; the launch traced here: 70.2 us
  Pallas kernels  67 us (95%)
  local copies, waits for them, and re-layouts  3.15 us (4%)
    pallas_call x1, Pallas kernels, local(): pl.pallas_call(kernel, out_shape=jax.ShapeDtypeStruct((FR, 4 * FR), F32),...  67 us
    unnamed x5, local copies, waits for them, and re-layouts  3.15 us

profile of v2, /device:TPU:1, one launch (start us, length us, event | category | flops | bytes accessed | tf_op | source)
XLA Modules:
  0.0 70.2 jit_solution(14668163516677460919)
XLA Ops:
  0.0 0.0 copy-start
  0.0 1.1 %copy-done = f32[384,384]{1,0:T(8,128)S(1)} copy-done((f32[384,384]{1,0:T(8,128)S(1)}, f32[384,384]{1,0:T(8,128)}, u32[]{:S(2)}) %copy-start) | copy-done | bytes 589848
  1.1 0.0 copy-start.1
  1.1 0.7 copy-done.1
  1.7 67.0 %shard_map.28 = f32[384,1536]{1,0:T(8,128)S(1)} custom-call(f32[384,384]{1,0:T(8,128)S(1)} %copy-done, s32[1,192]{1,0:T(1,128)S(1)} %bitcast.1), custom_call_target="tpu_custom_call" | custom-call | tf_op jit(solution)/shard_map/pallas_call | solution.py:289
  68.8 1.4 %copy.4 = f32[384,1536]{1,0:T(8,128)} copy(f32[384,1536]{1,0:T(8,128)S(1)} %shard_map.28) | data formatting | bytes 4718592
Async XLA Ops:
  0.0 1.1 %copy-start = (f32[384,384]{1,0:T(8,128)S(1)}, f32[384,384]{1,0:T(8,128)}, u32[]{:S(2)}) copy-start(f32[384,384]{1,0:T(8,128)} %lib_ref.1) | copy-start | bytes 1769476
  1.1 0.7 copy-start.1

commit v3 on v2

--- a/solution.py
+++ b/solution.py
@@ -11,7 +11,8 @@
 SL = 24
 ROWS = NZ * SL
 FR = 384
-NA = 4
+EARLY = ((0, 8), (8, 16))
+NA = 3
 EPS = 1e-06
 MESH = pl.DeviceIdType.MESH
 F32 = jnp.float32
@@ -34,7 +35,7 @@
 def kernel(
     lib_ref, ann_ref, out_ref,
     piece, rows, cols, acc, mu, s1, s2, rmean, rscale,
-    snd, move, ag0, ag1, bex, rowsem, rowlow, sibrow, outsem, outsnd,
+    snd, move, ag0, farsem, swap, ag1, bex, rowsem, rowlow, sibrow, outsem, outsnd,
 ):
     f = lax.axis_index("frame")
     p = lax.axis_index("pix")
@@ -93,58 +94,71 @@
     def wait(like, sem):
         pltpu.make_async_copy(like, like, sem).wait()
 
-    def scatter():
+    def scatter(g):
+        span = pl.ds(*EARLY[g])
         for d in (4, 3, 5, 2, 6, 1, 7):
             w = (z + d) % NZ
-            send(piece.at[w], cols.at[w, 0, p], snd.at[0], move, target(w))
+            send(piece.at[w, span], cols.at[w, 0, p, span], snd.at[0], move.at[g], target(w))
 
         @pl.when(z != p)
         def _():
-            send(piece.at[z], cols.at[z, 0, p], snd.at[0], move, target(z))
+            send(piece.at[z, span], cols.at[z, 0, p, span], snd.at[0], move.at[g], target(z))
 
         @pl.when(z == p)
         def _():
-            pltpu.make_async_copy(piece.at[z], cols.at[z, 0, p], move).start()
-
-    def own(j):
-        return cols.at[j, 0]
-
-    def also(j):
-        return cols.at[j, 1, pl.ds(0, NA)]
-
-    def forward0(j, d):
-        send(own(j), own(j), snd.at[4], ag0.at[j], at(dz=d))
-
-    def forward1(j, d):
-        send(also(j), also(j), snd.at[5], ag1.at[j], at(dz=d))
+            pltpu.make_async_copy(piece.at[z, span], cols.at[z, 0, p, span], move.at[g]).start()
+
+    late, soon = pl.ds(NA, NPIX - NA), pl.ds(0, NA)
+
+    def b(j):
+        return cols.at[j, 0, late]
+
+    def a(j):
+        return cols.at[j, :, soon]
 
     def cross(j):
-        rest = pl.ds(NA, NPIX - NA)
-        send(cols.at[j, 0, rest], cols.at[j, 1, rest], snd.at[6], bex.at[j], partner)
+        send(b(j), cols.at[j, 1, late], snd.at[6], bex.at[j], partner)
 
     def begin():
-        wait(own(z), move)
-        forward0(z, 1)
-        forward0(z, 7)
-        send(cols.at[z, 0, pl.ds(0, NA)], also(z), snd.at[3], ag1.at[z], partner)
+        for g in range(len(EARLY)):
+            span = pl.ds(*EARLY[g])
+            wait(cols.at[z, 0, :, span], move.at[g])
+            part = cols.at[z, 0, late, span]
+            for d in (1, 7):
+                send(part, part, snd.at[4], ag0.at[z], at(dz=d))
+        send(cols.at[z, 0, soon], cols.at[z, 1, soon], snd.at[3], swap, partner)
         cross(z)
-        wait(also(z), ag1.at[z])
-        forward1(z, 1)
-        forward1(z, 7)
-
-    def arrive(t):
-        below, above = (z + NZ - t) % NZ, (z + t) % NZ
-        for view, sem, fwd in ((own, ag0, forward0), (also, ag1, forward1)):
-            for j, d, core in ((below, 1, 0), (above, 7, 1)):
-                wait(view(j), sem.at[j])
-                if t < 3:
-                    fwd(j, d)
-                else:
-                    @pl.when(c == core)
-                    def _():
-                        fwd(j, d)
-                if view is own:
-                    cross(j)
+
+    def swapped():
+        wait(cols.at[z, 1, soon], swap)
+        for d in (1, 7):
+            send(a(z), a(z), snd.at[5], ag1.at[z], at(dz=d))
+
+    def ends(t):
+        return ((z + NZ - t) % NZ, 1, 0), ((z + t) % NZ, 7, 1)
+
+    def arrive_b(t):
+        for j, d, core in ends(t):
+            wait(b(j), ag0.at[j])
+            if t < 3:
+                send(b(j), b(j), snd.at[4], ag0.at[j], at(dz=d))
+            else:
+                @pl.when(c == core)
+                def _():
+                    send(b(j), b(j), snd.at[4], ag0.at[j], at(dz=d))
+            cross(j)
+
+    def arrive_a(t):
+        for j, d, core in ends(t):
+            wait(a(j), ag1.at[j])
+            if t < 3:
+                send(a(j), a(j), snd.at[5], ag1.at[j], at(dz=d))
+            else:
+                @pl.when(c == core)
+                def _():
+                    for h in range(2):
+                        part = cols.at[j, h, soon]
+                        send(part, part, snd.at[5], farsem.at[h], at(dz=d))
 
     def row(k):
         return rows.at[c, :, k]
@@ -173,7 +187,8 @@
         wait(rows.at[c, pl.ds(4, 4), k], rowlow.at[k])
         share(k)
 
-    scatter()
+    for g in range(len(EARLY)):
+        scatter(g)
     send(piece, row(p), snd.at[1], rowsem.at[p], flip)
     both(piece, p)
     send(piece, row(p), snd.at[2], sibrow, sibling)
@@ -182,10 +197,13 @@
     both(row(pf), pf)
     share(pf)
     pass_on(yl)
-    arrive(1)
+    arrive_b(1)
+    swapped()
     pass_on(1 - yl)
+    arrive_b(2)
     last(yl)
-    arrive(2)
+    arrive_a(1)
+    arrive_b(3)
     last(1 - yl)
     wait(rows.at[0], sibrow)
 
@@ -216,7 +234,7 @@
 
     def product(j, hs, first=False):
         if 1 in hs:
-            wait(cols.at[j, 1, pl.ds(NA, NPIX - NA)], bex.at[j])
+            wait(cols.at[j, 1, late], bex.at[j])
         pairs = [shifted(j, h, first) for h in hs]
         xhi, xlo = (jnp.concatenate(v, axis=1) for v in zip(*pairs))
         for k in range(2):
@@ -254,15 +272,17 @@
 
     far = (z + 4) % NZ
     product(z, (0, 1), True)
+    arrive_a(2)
+    wait(b(far), ag0.at[far])
+    cross(far)
     pair(1)
-    arrive(3)
     pair(2)
-    wait(own(far), ag0.at[far])
-    cross(far)
+    arrive_a(3)
     pair(3)
+    wait(cols.at[far, 0, soon], farsem.at[0])
     product(far, (0,))
     output(0)
-    wait(also(far), ag1.at[far])
+    wait(cols.at[far, 1, soon], farsem.at[1])
     product(far, (1,))
     output(1)
     for theirs, mine in copies:
@@ -278,10 +298,10 @@
     wait(cols.at[pl.ds(0, 7), 0], snd.at[1])
     wait(cols.at[:, 0], snd.at[2])
 
-    wait(also(0), snd.at[3])
-    wait(cols.at[pl.ds(0, 7), 0], snd.at[4])
-    wait(cols.at[pl.ds(0, 7), 0, pl.ds(0, NA)], snd.at[5])
-    wait(cols.at[:, 0, pl.ds(0, NPIX - NA)], snd.at[6])
+    wait(cols.at[0, 0, soon], snd.at[3])
+    wait(cols.at[pl.ds(0, 7), 0, late], snd.at[4])
+    wait(cols.at[pl.ds(0, 7), :, soon], snd.at[5])
+    wait(cols.at[:, 0, late], snd.at[6])
 
 
 def local(library, annulus):
@@ -302,8 +322,10 @@
             pltpu.VMEM((2, 1, FR), F32),
             pltpu.VMEM((2, 1, FR), F32),
             dma((7,)),
+            dma((len(EARLY),)),
+            dma((NZ,)),
+            dma((2,)),
             dma,
-            dma((NZ,)),
             dma((NZ,)),
             dma((NZ,)),
             dma((NPIX,)),

time: 70.3 us -> 63.7 us (0.906)
  Pallas kernels: 67 us -> 60.4 us
    pallas_call x1, Pallas kernels: 67 us -> 60.4 us  [local(): pl.pallas_call(kernel, out_shape=jax.ShapeDtypeStruct((FR, 4 * FR), F32),...]
where the time goes in v3:
time: 63.7 us; the launch traced here: 63.6 us
  Pallas kernels  60.4 us (95%)
  local copies, waits for them, and re-layouts  3.15 us (5%)
    pallas_call x1, Pallas kernels, local(): pl.pallas_call(kernel, out_shape=jax.ShapeDtypeStruct((FR, 4 * FR), F32),...  60.4 us
    unnamed x5, local copies, waits for them, and re-layouts  3.15 us

profile of v3, /device:TPU:1, one launch (start us, length us, event | category | flops | bytes accessed | tf_op | source)
XLA Modules:
  0.0 63.6 jit_solution(15880482453476284723)
XLA Ops:
  0.0 0.0 copy-start
  0.0 1.1 %copy-done = f32[384,384]{1,0:T(8,128)S(1)} copy-done((f32[384,384]{1,0:T(8,128)S(1)}, f32[384,384]{1,0:T(8,128)}, u32[]{:S(2)}) %copy-start) | copy-done | bytes 589848
  1.1 0.0 copy-start.1
  1.1 0.7 %copy-done.1 = s32[192]{0:T(256)S(1)} copy-done((s32[192]{0:T(256)S(1)}, s32[192]{0:T(256)}, u32[]{:S(2)}) %copy-start.1) | copy-done | bytes 792
  1.7 60.4 %shard_map.28 = f32[384,1536]{1,0:T(8,128)S(1)} custom-call(f32[384,384]{1,0:T(8,128)S(1)} %copy-done, s32[1,192]{1,0:T(1,128)S(1)} %bitcast.1), custom_call_target="tpu_custom_call" | custom-call | tf_op jit(solution)/shard_map/pallas_call | solution.py:309
  62.2 1.4 %copy.4 = f32[384,1536]{1,0:T(8,128)} copy(f32[384,1536]{1,0:T(8,128)S(1)} %shard_map.28) | data formatting | bytes 4718592
Async XLA Ops:
  0.0 1.1 %copy-start = (f32[384,384]{1,0:T(8,128)S(1)}, f32[384,384]{1,0:T(8,128)}, u32[]{:S(2)}) copy-start(f32[384,384]{1,0:T(8,128)} %lib_ref.1) | copy-start | bytes 1769476
  1.1 0.7 %copy-start.1 = (s32[192]{0:T(256)S(1)}, s32[192]{0:T(256)}, u32[]{:S(2)}) copy-start(s32[192]{0:T(256)} %param.3) | copy-start | bytes 2308

commit v4 on v3

v4 whole, which is shorter than its diff:
```python
import jax
import jax.numpy as jnp
from jax import lax
from jax.experimental import pallas as pl
from jax.experimental.pallas import tpu as pltpu
from jax.sharding import PartitionSpec as P

PIX = 1536
NZ = 8
NPIX = 8
SL = 24
ROWS = NZ * SL
FR = 384
EARLY = ((0, 8), (8, 16))
NA = (4, 3)
EPS = 1e-06
MESH = pl.DeviceIdType.MESH
F32 = jnp.float32
BF16 = jnp.bfloat16


def device(x, y, z, c):
    return (z * 4 + (y // 2) * 2 + c, x * 2 + y % 2)


def split(v):
    hi = v.astype(BF16)
    return hi, (v - hi.astype(F32)).astype(BF16)


def dot(a, b):
    return lax.dot_general(a, b, (((1,), (0,)), ((), ())), preferred_element_type=F32)


def kernel(
    lib_ref, ann_ref, out_ref,
    piece, rows, cols, acc, left, mu, s1, s2, rmean, rscale,
    snd, move, ag0, swap, ag1, bex, rowsem, rowlow, sibrow, outsem, outsnd,
):
    f = lax.axis_index("frame")
    p = lax.axis_index("pix")
    z, yh, c = f // 4, (f // 2) % 2, f % 2
    x, yl = p // 2, p % 2
    y = 2 * yh + yl

    def at(dx=0, dy=0, dz=0, dc=0):
        return device((x + dx) % 4, (y + dy) % 4, (z + dz) % NZ, (c + dc) % 2)

    sibling = at(dc=1)
    partner = at(dy=2)
    flip = device(x, 2 * yh + 1 - yl, z, c)
    pf = 2 * x + 1 - yl

    barrier = pltpu.get_barrier_semaphore()
    def greet(to):
        pl.semaphore_signal(barrier, inc=1, device_id=to, device_id_type=MESH)

    def target(w):
        return device(z // 2, z % 2 + 2 * yh, w, c)

    for k in range(NPIX):
        @pl.when((k != p) | (z != p))
        def _():
            greet(device(k // 2, 2 * yh + k % 2, p, c))
    for to in (at(dz=1), at(dz=7), at(dx=1), at(dx=3), flip, partner, sibling):
        greet(to)

    band = lax.broadcasted_iota(jnp.int32, (FR, ROWS), 0)
    onehot = jnp.where(band == ann_ref[...], 1.0, 0.0).astype(F32).T.astype(BF16)
    lib = lib_ref[...]
    hi = lib.astype(BF16)
    rest = lib - hi.astype(F32)
    mid = rest.astype(BF16)
    low = (rest - mid.astype(F32)).astype(BF16)
    nt = (((1,), (1,)), ((), ()))
    picked = lax.dot_general(onehot, hi, nt, preferred_element_type=F32)
    picked += lax.dot_general(onehot, mid, nt, preferred_element_type=F32)
    picked += lax.dot_general(onehot, low, nt, preferred_element_type=F32)
    picked = picked.reshape(NZ, SL, FR)
    piece[...] = picked
    rows[c, :, p] = picked

    pl.semaphore_wait(barrier, 7 + NZ - jnp.where(z == p, 1, 0))

    def send(src, dst, out, into, to):
        pltpu.make_async_remote_copy(
            src_ref=src, dst_ref=dst, send_sem=out, recv_sem=into, device_id=to, device_id_type=MESH
        ).start()

    def wait(like, sem):
        pltpu.make_async_copy(like, like, sem).wait()

    def scatter(g):
        span = pl.ds(*EARLY[g])
        for d in (4, 3, 5, 2, 6, 1, 7):
            w = (z + d) % NZ
            send(piece.at[w, span], cols.at[w, 0, p, span], snd.at[0], move.at[g], target(w))

        @pl.when(z != p)
        def _():
            send(piece.at[z, span], cols.at[z, 0, p, span], snd.at[0], move.at[g], target(z))

        @pl.when(z == p)
        def _():
            pltpu.make_async_copy(piece.at[z, span], cols.at[z, 0, p, span], move.at[g]).start()

    def cases(act):
        for core in range(2):
            @pl.when(c == core)
            def _():
                act(pl.ds(0, NA[core]), pl.ds(NA[core], NPIX - NA[core]))

    def cross(j, late, span=pl.ds(0, SL)):
        send(cols.at[j, 0, late, span], cols.at[j, 1, late, span], snd.at[6], bex.at[j], partner)

    def begin(soon, late):
        for g in range(len(EARLY)):
            span = pl.ds(*EARLY[g])
            wait(cols.at[z, 0, :, span], move.at[g])
            part = cols.at[z, 0, late, span]
            for d in (1, 7):
                send(part, part, snd.at[4], ag0.at[z], at(dz=d))
            send(cols.at[z, 0, soon, span], cols.at[z, 1, soon, span], snd.at[3], swap.at[g], partner)
            cross(z, late, span)

    def swapped(g):
        def act(soon, late):
            span = pl.ds(*EARLY[g])
            wait(cols.at[z, 1, soon, span], swap.at[g])
            a = cols.at[z, :, soon, span]
            for d in (1, 7):
                send(a, a, snd.at[5], ag1.at[0, z], at(dz=d))
        cases(act)

    def ends(t):
        return ((z + NZ - t) % NZ, 1), ((z + t) % NZ, 7)

    def arrive_b(t):
        def act(soon, late):
            for i, (j, d) in enumerate(ends(t)):
                b = cols.at[j, 0, late]
                wait(b, ag0.at[j])
                if t == 3:
                    n = late.size // 2
                    b = cols.at[j, 0, pl.ds(late.start + i * n, n if i == 0 else late.size - n)]
                send(b, b, snd.at[4], ag0.at[j], at(dz=d))
                cross(j, late)
        cases(act)

    def arrive_a(t):
        def act(soon, late):
            if t == 1:
                for j, d in ends(t):
                    a = cols.at[j, :, soon]
                    wait(a, ag1.at[0, j])
                    send(a, a, snd.at[5], ag1.at[0, j], at(dz=d))
            elif t == 2:
                for i, (j, d) in enumerate(ends(t)):
                    wait(cols.at[j, :, soon], ag1.at[0, j])
                    for h in (i, 1 - i):
                        a = cols.at[j, h, soon]
                        send(a, a, snd.at[5], ag1.at[h, j], at(dz=d))
            else:
                for k in range(2):
                    for i, (j, d) in enumerate(ends(t)):
                        h = i ^ k
                        a = cols.at[j, h, soon]
                        wait(a, ag1.at[h, j])
                        if k == 0:
                            send(a, a, snd.at[5], ag1.at[h, j], at(dz=d))
        cases(act)

    def arrive_far(soon, late):
        wait(cols.at[far, 0, late], ag0.at[far])
        cross(far, late)

    def crossed(j):
        cases(lambda soon, late: wait(cols.at[j, 1, late], bex.at[j]))

    def arrived(h):
        cases(lambda soon, late: wait(cols.at[far, h, soon], ag1.at[h, far]))

    far = (z + 4) % NZ

    def row(k):
        return rows.at[c, :, k]

    def share(k):
        send(row(k), row(k), snd.at[2], sibrow, sibling)

    def both(src, k):
        for d in (1, 3):
            send(src, row(k), snd.at[1], rowsem.at[k], at(dx=d))

    def pass_on(q):
        left, right = 2 * ((x + 3) % 4) + q, 2 * ((x + 1) % 4) + q
        wait(row(left), rowsem.at[left])
        top = rows.at[c, pl.ds(0, 4), left]
        send(top, top, snd.at[1], rowsem.at[left], at(dx=1))
        share(left)
        wait(row(right), rowsem.at[right])
        low = rows.at[c, pl.ds(4, 4), right]
        send(low, low, snd.at[1], rowlow.at[right], at(dx=3))
        share(right)

    def last(q):
        k = 2 * ((x + 2) % 4) + q
        wait(rows.at[c, pl.ds(0, 4), k], rowsem.at[k])
        wait(rows.at[c, pl.ds(4, 4), k], rowlow.at[k])
        share(k)

    def block(ref, *idx):
        return ref[idx].reshape(ROWS, FR)

    def stats():
        last(1 - yl)
        wait(rows.at[0], sibrow)
        for k in range(2):
            def add(j, tot):
                return tot + jnp.sum(block(rows, k, j), axis=0, keepdims=True)

            mean = lax.fori_loop(0, NZ, add, jnp.zeros((1, FR), F32)) / PIX

            def add2(j, tot):
                v = block(rows, k, j) - mean
                return tot + jnp.sum(v * v, axis=0, keepdims=True)

            sq = lax.fori_loop(0, NZ, add2, jnp.zeros((1, FR), F32))
            rmean[k] = mean
            rscale[k] = 1.0 / jnp.sqrt(sq + EPS)

    def shifted(j, h, first):
        v = block(cols, j, h)
        if first:
            mu[h] = jnp.sum(v, axis=0, keepdims=True) / ROWS
        v = v - mu[h]
        one = jnp.sum(v, axis=0, keepdims=True)
        two = jnp.sum(v * v, axis=0, keepdims=True)
        s1[h] = one if first else s1[h] + one
        s2[h] = two if first else s2[h] + two
        return split(v)

    def unit(k, j):
        return [v.T for v in split((block(rows, k, j) - rmean[k]) * rscale[k])]

    def product(j, hs, first=False, final=False):
        if 1 in hs:
            crossed(j)
        pairs = [shifted(j, h, first) for h in hs]
        xhi, xlo = (jnp.concatenate(v, axis=1) for v in zip(*pairs))
        if final:
            (h,) = hs
            m = s1[h] / PIX
            sq = jnp.maximum(s2[h] - PIX * m * m, 0.0)
            scale = 1.0 / jnp.sqrt(sq + EPS)
            col = pl.multiple_of((2 * (yh if h == 0 else 1 - yh) + c) * FR, 128)
            here = out_ref.at[:, pl.ds(col, FR)]
        for k in (1 - c, c) if final else range(2):
            if final:
                uhi, ulo = left[0, k], left[1, k]
            else:
                uhi, ulo = unit(k, j)
            r = dot(uhi, xhi) + dot(uhi, xlo) + dot(ulo, xhi)
            if final:
                acc[h, k] = (acc[h, k] + r) * scale
                if k is c:
                    copy = pltpu.make_async_copy(acc.at[h, k], here, outsnd.at[2 + h])
                else:
                    copy = pltpu.make_async_remote_copy(
                        src_ref=acc.at[h, k], dst_ref=here, send_sem=outsnd.at[h], recv_sem=outsem.at[h],
                        device_id=sibling, device_id_type=MESH,
                    )
                copy.start()
                copies.append(copy)
                continue
            for i, h in enumerate(hs):
                r_h = r[:, i * FR : (i + 1) * FR]
                acc[h, k] = r_h if first else acc[h, k] + r_h

    def pair(t):
        @pl.loop(0, 2)
        def _(i):
            product((z + jnp.where(i == 0, t, NZ - t)) % NZ, (0, 1))

    copies = []
    for g in range(len(EARLY)):
        scatter(g)
    send(piece, row(p), snd.at[1], rowsem.at[p], flip)
    both(piece, p)
    send(piece, row(p), snd.at[2], sibrow, sibling)
    cases(begin)
    wait(row(pf), rowsem.at[pf])
    both(row(pf), pf)
    share(pf)
    pass_on(yl)
    swapped(0)
    arrive_b(1)
    for g in range(1, len(EARLY)):
        swapped(g)
    pass_on(1 - yl)
    arrive_b(2)
    last(yl)
    arrive_a(1)
    stats()
    product(z, (0, 1), True)
    arrive_b(3)
    pair(1)
    arrive_a(2)
    cases(arrive_far)
    pair(2)
    arrive_a(3)
    pair(3)
    for k in range(2):
        left[0, k], left[1, k] = unit(k, far)
    arrived(0)
    product(far, (0,), final=True)
    arrived(1)
    product(far, (1,), final=True)
    for copy in copies:
        copy.wait()

    wait(cols.at[0, 0, pl.ds(0, 7)], snd.at[0])

    @pl.when(z != p)
    def _():
        wait(piece.at[0], snd.at[0])

    wait(cols.at[pl.ds(0, 7), 0], snd.at[1])
    wait(cols.at[:, 0], snd.at[2])

    def sent(soon, late):
        wait(cols.at[0, 0, soon], snd.at[3])
        wait(cols.at[pl.ds(0, 7), 0, late], snd.at[4])
        wait(cols.at[pl.ds(0, 7), :, soon], snd.at[5])
        wait(cols.at[:, 0, late], snd.at[6])

    cases(sent)


def local(library, annulus):
    dma = pltpu.SemaphoreType.DMA
    return pl.pallas_call(
        kernel,
        out_shape=jax.ShapeDtypeStruct((FR, 4 * FR), F32),
        in_specs=[pl.BlockSpec(memory_space=pltpu.VMEM)] * 2,
        out_specs=pl.BlockSpec(memory_space=pl.ANY),
        scratch_shapes=[
            pltpu.VMEM((NZ, SL, FR), F32),
            pltpu.VMEM((2, NZ, NPIX, SL, FR), F32),
            pltpu.VMEM((NZ, 2, NPIX, SL, FR), F32),
            pltpu.VMEM((2, 2, FR, FR), F32),
            pltpu.VMEM((2, 2, FR, ROWS), BF16),
            pltpu.VMEM((2, 1, FR), F32),
            pltpu.VMEM((2, 1, FR), F32),
            pltpu.VMEM((2, 1, FR), F32),
            pltpu.VMEM((2, 1, FR), F32),
            pltpu.VMEM((2, 1, FR), F32),
            dma((7,)),
            dma((len(EARLY),)),
            dma((NZ,)),
            dma((len(EARLY),)),
            dma((2, NZ)),
            dma((NZ,)),
            dma((NPIX,)),
            dma((NPIX,)),
            dma,
            dma((2,)),
            dma((4,)),
        ],
        compiler_params=pltpu.CompilerParams(
            collective_id=0, has_side_effects=True, vmem_limit_bytes=48 * 2**20
        ),
    )(library, annulus.reshape(1, ROWS))


def solution(mesh):
    placed = (P("frame", "pix"), P("pix"))
    return jax.shard_map(
        local, mesh=mesh, in_specs=placed, out_specs=P("frame", "pix"), check_vma=False
    )
```

time: 63.7 us -> 61.3 us (0.962)
  Pallas kernels: 60.4 us -> 58 us
    pallas_call x1, Pallas kernels: 60.4 us -> 58 us  [local(): pl.pallas_call(kernel, out_shape=jax.ShapeDtypeStruct((FR, 4 * FR), F32),...]
where the time goes in v4:
time: 61.3 us; the launch traced here: 61.1 us
  Pallas kernels  58 us (95%)
  local copies, waits for them, and re-layouts  3.15 us (5%)
    pallas_call x1, Pallas kernels, local(): pl.pallas_call(kernel, out_shape=jax.ShapeDtypeStruct((FR, 4 * FR), F32),...  58 us
    unnamed x5, local copies, waits for them, and re-layouts  3.15 us

profile of v4, /device:TPU:1, one launch (start us, length us, event | category | flops | bytes accessed | tf_op | source)
XLA Modules:
  0.0 61.1 jit_solution(5852506052683283952)
XLA Ops:
  0.0 0.0 copy-start
  0.0 1.1 %copy-done = f32[384,384]{1,0:T(8,128)S(1)} copy-done((f32[384,384]{1,0:T(8,128)S(1)}, f32[384,384]{1,0:T(8,128)}, u32[]{:S(2)}) %copy-start) | copy-done | bytes 589848
  1.1 0.0 copy-start.1
  1.1 0.7 %copy-done.1 = s32[192]{0:T(256)S(1)} copy-done((s32[192]{0:T(256)S(1)}, s32[192]{0:T(256)}, u32[]{:S(2)}) %copy-start.1) | copy-done | bytes 792
  1.7 58.0 %shard_map.28 = f32[384,1536]{1,0:T(8,128)S(1)} custom-call(f32[384,384]{1,0:T(8,128)S(1)} %copy-done, s32[1,192]{1,0:T(1,128)S(1)} %bitcast.1), custom_call_target="tpu_custom_call" | custom-call | tf_op jit(solution)/shard_map/pallas_call | solution.py:342
  59.7 1.4 %copy.4 = f32[384,1536]{1,0:T(8,128)} copy(f32[384,1536]{1,0:T(8,128)S(1)} %shard_map.28) | data formatting | bytes 4718592
Async XLA Ops:
  0.0 1.1 %copy-start = (f32[384,384]{1,0:T(8,128)S(1)}, f32[384,384]{1,0:T(8,128)}, u32[]{:S(2)}) copy-start(f32[384,384]{1,0:T(8,128)} %lib_ref.1) | copy-start | bytes 1769476
  1.1 0.7 %copy-start.1 = (s32[192]{0:T(256)S(1)}, s32[192]{0:T(256)}, u32[]{:S(2)}) copy-start(s32[192]{0:T(256)} %param.3) | copy-start | bytes 2308

commit v5 on v4

--- a/solution.py
+++ b/solution.py
@@ -65,8 +65,9 @@
     for to in (at(dz=1), at(dz=7), at(dx=1), at(dx=3), flip, partner, sibling):
         greet(to)
 
-    band = lax.broadcasted_iota(jnp.int32, (FR, ROWS), 0)
-    onehot = jnp.where(band == ann_ref[...], 1.0, 0.0).astype(F32).T.astype(BF16)
+    band = lax.broadcasted_iota(jnp.int32, (ROWS, FR), 1)
+    want = jnp.broadcast_to(ann_ref[...], (8, ROWS)).T[:, :1]
+    onehot = jnp.where(band == want, 1.0, 0.0).astype(BF16)
     lib = lib_ref[...]
     hi = lib.astype(BF16)
     rest = lib - hi.astype(F32)
@@ -120,17 +121,18 @@
             part = cols.at[z, 0, late, span]
             for d in (1, 7):
                 send(part, part, snd.at[4], ag0.at[z], at(dz=d))
-            send(cols.at[z, 0, soon, span], cols.at[z, 1, soon, span], snd.at[3], swap.at[g], partner)
+            send(cols.at[z, 0, soon, span], cols.at[z, 1, soon, span], snd.at[3], swap, partner)
             cross(z, late, span)
-
-    def swapped(g):
-        def act(soon, late):
-            span = pl.ds(*EARLY[g])
-            wait(cols.at[z, 1, soon, span], swap.at[g])
-            a = cols.at[z, :, soon, span]
-            for d in (1, 7):
-                send(a, a, snd.at[5], ag1.at[0, z], at(dz=d))
-        cases(act)
+        pass_a(z, 0, soon, (1, 7))
+
+    def pass_a(j, h, soon, ds):
+        a = cols.at[j, h, soon]
+        for d in ds:
+            send(a, a, snd.at[5], ag1.at[h, j], at(dz=d))
+
+    def swapped(soon, late):
+        wait(cols.at[z, 1, soon], swap)
+        pass_a(z, 1, soon, (1, 7))
 
     def ends(t):
         return ((z + NZ - t) % NZ, 1), ((z + t) % NZ, 7)
@@ -147,27 +149,12 @@
                 cross(j, late)
         cases(act)
 
-    def arrive_a(t):
+    def arrive_a(t, h):
         def act(soon, late):
-            if t == 1:
-                for j, d in ends(t):
-                    a = cols.at[j, :, soon]
-                    wait(a, ag1.at[0, j])
-                    send(a, a, snd.at[5], ag1.at[0, j], at(dz=d))
-            elif t == 2:
-                for i, (j, d) in enumerate(ends(t)):
-                    wait(cols.at[j, :, soon], ag1.at[0, j])
-                    for h in (i, 1 - i):
-                        a = cols.at[j, h, soon]
-                        send(a, a, snd.at[5], ag1.at[h, j], at(dz=d))
-            else:
-                for k in range(2):
-                    for i, (j, d) in enumerate(ends(t)):
-                        h = i ^ k
-                        a = cols.at[j, h, soon]
-                        wait(a, ag1.at[h, j])
-                        if k == 0:
-                            send(a, a, snd.at[5], ag1.at[h, j], at(dz=d))
+            for i, (j, d) in enumerate(ends(t)):
+                wait(cols.at[j, h, soon], ag1.at[h, j])
+                if t < 3 or i == h:
+                    pass_a(j, h, soon, (d,))
         cases(act)
 
     def arrive_far(soon, late):
@@ -293,25 +280,26 @@
     both(row(pf), pf)
     share(pf)
     pass_on(yl)
-    swapped(0)
     arrive_b(1)
-    for g in range(1, len(EARLY)):
-        swapped(g)
+    cases(swapped)
     pass_on(1 - yl)
     arrive_b(2)
     last(yl)
-    arrive_a(1)
+    arrive_a(1, 0)
+    arrive_a(1, 1)
     stats()
     product(z, (0, 1), True)
     arrive_b(3)
     pair(1)
-    arrive_a(2)
+    arrive_a(2, 0)
+    arrive_a(2, 1)
     cases(arrive_far)
     pair(2)
-    arrive_a(3)
-    pair(3)
+    arrive_a(3, 0)
+    arrive_a(3, 1)
     for k in range(2):
         left[0, k], left[1, k] = unit(k, far)
+    pair(3)
     arrived(0)
     product(far, (0,), final=True)
     arrived(1)
@@ -358,7 +346,7 @@
             dma((7,)),
             dma((len(EARLY),)),
             dma((NZ,)),
-            dma((len(EARLY),)),
+            dma,
             dma((2, NZ)),
             dma((NZ,)),
             dma((NPIX,)),

time: 61.3 us -> 60.8 us (level)
  no operation moved by 1% of the time
where the time goes in v5:
time: 60.8 us; the launch traced here: 60.6 us
  Pallas kernels  57.5 us (95%)
  local copies, waits for them, and re-layouts  3.15 us (5%)
    pallas_call x1, Pallas kernels, local(): pl.pallas_call(kernel, out_shape=jax.ShapeDtypeStruct((FR, 4 * FR), F32),...  57.5 us
    unnamed x5, local copies, waits for them, and re-layouts  3.15 us

profile of v5, /device:TPU:1, one launch (start us, length us, event | category | flops | bytes accessed | tf_op | source)
XLA Modules:
  0.0 60.6 jit_solution(14069272038710587435)
XLA Ops:
  0.0 0.0 copy-start
  0.0 1.1 %copy-done = f32[384,384]{1,0:T(8,128)S(1)} copy-done((f32[384,384]{1,0:T(8,128)S(1)}, f32[384,384]{1,0:T(8,128)}, u32[]{:S(2)}) %copy-start) | copy-done | bytes 589848
  1.1 0.0 copy-start.1
  1.1 0.7 %copy-done.1 = s32[192]{0:T(256)S(1)} copy-done((s32[192]{0:T(256)S(1)}, s32[192]{0:T(256)}, u32[]{:S(2)}) %copy-start.1) | copy-done | bytes 792
  1.7 57.5 %shard_map.28 = f32[384,1536]{1,0:T(8,128)S(1)} custom-call(f32[384,384]{1,0:T(8,128)S(1)} %copy-done, s32[1,192]{1,0:T(1,128)S(1)} %bitcast.1), custom_call_target="tpu_custom_call" | custom-call | tf_op jit(solution)/shard_map/pallas_call | solution.py:330
  59.2 1.4 %copy.4 = f32[384,1536]{1,0:T(8,128)} copy(f32[384,1536]{1,0:T(8,128)S(1)} %shard_map.28) | data formatting | bytes 4718592
Async XLA Ops:
  0.0 1.1 %copy-start = (f32[384,384]{1,0:T(8,128)S(1)}, f32[384,384]{1,0:T(8,128)}, u32[]{:S(2)}) copy-start(f32[384,384]{1,0:T(8,128)} %lib_ref.1) | copy-start | bytes 1769476
  1.1 0.7 %copy-start.1 = (s32[192]{0:T(256)S(1)}, s32[192]{0:T(256)}, u32[]{:S(2)}) copy-start(s32[192]{0:T(256)} %param.3) | copy-start | bytes 2308

commit v6 on v5

--- a/solution.py
+++ b/solution.py
@@ -123,7 +123,15 @@
                 send(part, part, snd.at[4], ag0.at[z], at(dz=d))
             send(cols.at[z, 0, soon, span], cols.at[z, 1, soon, span], snd.at[3], swap, partner)
             cross(z, late, span)
-        pass_a(z, 0, soon, (1, 7))
+            if g == 0:
+                part = cols.at[z, 0, soon, span]
+                for d in (1, 7):
+                    send(part, part, snd.at[5], ag1.at[0, z], at(dz=d))
+
+        span = pl.ds(*EARLY[1])
+        part = cols.at[z, 0, soon, span]
+        for d in (1, 7):
+            send(part, part, snd.at[5], ag1.at[0, z], at(dz=d))
 
     def pass_a(j, h, soon, ds):
         a = cols.at[j, h, soon]

time: 60.8 us -> 60.6 us (level)
  no operation moved by 1% of the time
where the time goes in v6:
time: 60.6 us; the launch traced here: 60.5 us
  Pallas kernels  57.3 us (95%)
  local copies, waits for them, and re-layouts  3.15 us (5%)
    pallas_call x1, Pallas kernels, local(): pl.pallas_call(kernel, out_shape=jax.ShapeDtypeStruct((FR, 4 * FR), F32),...  57.3 us
    unnamed x5, local copies, waits for them, and re-layouts  3.15 us

profile of v6, /device:TPU:1, one launch (start us, length us, event | category | flops | bytes accessed | tf_op | source)
XLA Modules:
  0.0 60.5 jit_solution(13036985188669224317)
XLA Ops:
  0.0 0.0 copy-start
  0.0 1.1 %copy-done = f32[384,384]{1,0:T(8,128)S(1)} copy-done((f32[384,384]{1,0:T(8,128)S(1)}, f32[384,384]{1,0:T(8,128)}, u32[]{:S(2)}) %copy-start) | copy-done | bytes 589848
  1.1 0.0 copy-start.1
  1.1 0.7 %copy-done.1 = s32[192]{0:T(256)S(1)} copy-done((s32[192]{0:T(256)S(1)}, s32[192]{0:T(256)}, u32[]{:S(2)}) %copy-start.1) | copy-done | bytes 792
  1.7 57.3 %shard_map.28 = f32[384,1536]{1,0:T(8,128)S(1)} custom-call(f32[384,384]{1,0:T(8,128)S(1)} %copy-done, s32[1,192]{1,0:T(1,128)S(1)} %bitcast.1), custom_call_target="tpu_custom_call" | custom-call | tf_op jit(solution)/shard_map/pallas_call | solution.py:338
  59.1 1.4 %copy.4 = f32[384,1536]{1,0:T(8,128)} copy(f32[384,1536]{1,0:T(8,128)S(1)} %shard_map.28) | data formatting | bytes 4718592
Async XLA Ops:
  0.0 1.1 %copy-start = (f32[384,384]{1,0:T(8,128)S(1)}, f32[384,384]{1,0:T(8,128)}, u32[]{:S(2)}) copy-start(f32[384,384]{1,0:T(8,128)} %lib_ref.1) | copy-start | bytes 1769476
  1.1 0.7 %copy-start.1 = (s32[192]{0:T(256)S(1)}, s32[192]{0:T(256)}, u32[]{:S(2)}) copy-start(s32[192]{0:T(256)} %param.3) | copy-start | bytes 2308

commit v7 on v6

--- a/solution.py
+++ b/solution.py
@@ -308,6 +308,20 @@
     for k in range(2):
         left[0, k], left[1, k] = unit(k, far)
     pair(3)
+    wait(cols.at[0, 0, pl.ds(0, 7)], snd.at[0])
+
+    @pl.when(z != p)
+    def _():
+        wait(piece.at[0], snd.at[0])
+
+    wait(cols.at[pl.ds(0, 7), 0], snd.at[1])
+    wait(cols.at[:, 0], snd.at[2])
+
+    def sent(soon, late):
+        wait(cols.at[0, 0, soon], snd.at[3])
+        wait(cols.at[pl.ds(0, 7), 0, late], snd.at[4])
+
+    cases(sent)
     arrived(0)
     product(far, (0,), final=True)
     arrived(1)
@@ -315,22 +329,11 @@
     for copy in copies:
         copy.wait()
 
-    wait(cols.at[0, 0, pl.ds(0, 7)], snd.at[0])
-
-    @pl.when(z != p)
-    def _():
-        wait(piece.at[0], snd.at[0])
-
-    wait(cols.at[pl.ds(0, 7), 0], snd.at[1])
-    wait(cols.at[:, 0], snd.at[2])
-
-    def sent(soon, late):
-        wait(cols.at[0, 0, soon], snd.at[3])
-        wait(cols.at[pl.ds(0, 7), 0, late], snd.at[4])
+    def rest(soon, late):
         wait(cols.at[pl.ds(0, 7), :, soon], snd.at[5])
         wait(cols.at[:, 0, late], snd.at[6])
 
-    cases(sent)
+    cases(rest)
 
 
 def local(library, annulus):

time: 60.6 us -> 60.6 us (level)
  no operation moved by 1% of the time
where the time goes in v7:
time: 60.6 us; the launch traced here: 60.5 us
  Pallas kernels  57.3 us (95%)
  local copies, waits for them, and re-layouts  3.15 us (5%)
    pallas_call x1, Pallas kernels, local(): pl.pallas_call(kernel, out_shape=jax.ShapeDtypeStruct((FR, 4 * FR), F32),...  57.3 us
    unnamed x5, local copies, waits for them, and re-layouts  3.15 us

profile of v7, /device:TPU:1, one launch (start us, length us, event | category | flops | bytes accessed | tf_op | source)
XLA Modules:
  0.0 60.5 jit_solution(9328078377900466507)
XLA Ops:
  0.0 0.0 copy-start
  0.0 1.1 %copy-done = f32[384,384]{1,0:T(8,128)S(1)} copy-done((f32[384,384]{1,0:T(8,128)S(1)}, f32[384,384]{1,0:T(8,128)}, u32[]{:S(2)}) %copy-start) | copy-done | bytes 589848
  1.1 0.0 copy-start.1
  1.1 0.7 %copy-done.1 = s32[192]{0:T(256)S(1)} copy-done((s32[192]{0:T(256)S(1)}, s32[192]{0:T(256)}, u32[]{:S(2)}) %copy-start.1) | copy-done | bytes 792
  1.7 57.3 %shard_map.28 = f32[384,1536]{1,0:T(8,128)S(1)} custom-call(f32[384,384]{1,0:T(8,128)S(1)} %copy-done, s32[1,192]{1,0:T(1,128)S(1)} %bitcast.1), custom_call_target="tpu_custom_call" | custom-call | tf_op jit(solution)/shard_map/pallas_call | solution.py:341
  59.1 1.4 %copy.4 = f32[384,1536]{1,0:T(8,128)} copy(f32[384,1536]{1,0:T(8,128)S(1)} %shard_map.28) | data formatting | bytes 4718592
Async XLA Ops:
  0.0 1.1 %copy-start = (f32[384,384]{1,0:T(8,128)S(1)}, f32[384,384]{1,0:T(8,128)}, u32[]{:S(2)}) copy-start(f32[384,384]{1,0:T(8,128)} %lib_ref.1) | copy-start | bytes 1769476
  1.1 0.7 %copy-start.1 = (s32[192]{0:T(256)S(1)}, s32[192]{0:T(256)}, u32[]{:S(2)}) copy-start(s32[192]{0:T(256)} %param.3) | copy-start | bytes 2308
